TPU v7x, 32 devices: a whole 2x2x4 slice. The times are simulated.
32 devices in a mesh: group: 4 (over y, x), dev: 8 (over z, core).
Axes of the slice: x: 2, y: 2, z: 4, core: 2. Of those that a mesh axis runs over, the one named last changes fastest.
Arguments:
- embeddings: bfloat16 [40960, 768], P(('group', 'dev')), may hold values from -6 to 6
- projection: bfloat16 [256, 768], replicated, may hold values from -0.21875 to 0.21875
- triplets: int32 [3, 65536], P(None, ('group', 'dev')), may hold values from 0 to 1791, as said below
- cotangent: float32 [65536], P(('group', 'dev')), may hold values from -24 to 24
- wanted_rows: int32 [128, 128], P(('group', 'dev')), may hold values from -1 to 1279, as said below
Outputs:
- row_grad: bfloat16 [40960, 768], P(('group', 'dev'))
- weight_grad: float32 [256, 768], replicated
Inputs may be any that keep to these rules, and one draw needn't show every extreme that they name: `wanted_rows`: in each list the live entries come first and are distinct rows of the owning device, the rest are -1; each list holds from 128 // 4 (at least 1) to 128 live entries; all lists of some group of requesters are full, and all lists sent to some group are full. `triplets`: anchors are below 1280; a positive or negative below 1280 is one of the device's own rows, else 1280 + h * 128 + s names a live slot s of the device's list for group h.
All inputs are finite; a program needn't handle non-finite values.
Results may differ from a plain program's by a relative error of at most 0.0058.
Values may be sent and summed in bfloat16 or wider, within the bound.
A program may use at most 64 MiB of HBM per device.

v0:
```python
import math

import jax
import jax.numpy as jnp
from jax import lax
from jax.sharding import PartitionSpec as P

distance_scale = 0.0625
margin = 1.0
pull_share = 0.5


def triplet_gradients(lookup, triple, cotangent):
    anchor_rows = lookup[triple[0]].astype(jnp.float32)
    positive_rows = lookup[triple[1]].astype(jnp.float32)
    negative_rows = lookup[triple[2]].astype(jnp.float32)
    to_positive = anchor_rows - positive_rows
    to_negative = anchor_rows - negative_rows
    near = distance_scale * jnp.sum(to_positive * to_positive, axis=1)
    far = distance_scale * jnp.sum(to_negative * to_negative, axis=1)
    hinge_gate = jax.nn.sigmoid(margin + near - far)
    pull_factor = 2.0 * distance_scale * cotangent * (1.0 - pull_share + pull_share * hinge_gate)
    push_factor = 2.0 * distance_scale * cotangent * pull_share * hinge_gate
    pull_term = pull_factor[:, None] * to_positive
    push_term = push_factor[:, None] * to_negative
    gradient = jnp.zeros(lookup.shape, jnp.float32)
    gradient = gradient.at[triple[0]].add(pull_term - push_term)
    gradient = gradient.at[triple[1]].add(-pull_term)
    gradient = gradient.at[triple[2]].add(push_term)
    return gradient


def local(embeddings, projection, triplets, cotangent, wanted_rows):
    shard_rows = embeddings.shape[0]
    rank_width = projection.shape[0]
    groups = lax.axis_size("group")
    contract = (((1,), (1,)), ((), ()))
    own_projected = lax.dot_general(
        embeddings, projection, contract, preferred_element_type=jnp.float32
    ).astype(jnp.bfloat16)
    wanted = lax.all_to_all(wanted_rows, "group", split_axis=0, concat_axis=0, tiled=True)
    served_index = jnp.maximum(wanted, 0)
    served = own_projected[served_index]
    fetched = lax.all_to_all(served, "group", split_axis=0, concat_axis=0, tiled=True)
    lookup = jnp.concatenate([own_projected, fetched.reshape(-1, rank_width)], axis=0)
    gradient = triplet_gradients(lookup, triplets, cotangent)
    remote_grad = gradient[shard_rows:].reshape(groups, -1, rank_width).astype(jnp.bfloat16)
    returned = lax.all_to_all(remote_grad, "group", split_axis=0, concat_axis=0, tiled=True)
    row_total = (
        gradient[:shard_rows]
        .at[served_index.reshape(-1)]
        .add(returned.reshape(-1, rank_width).astype(jnp.float32))
    )
    row_rounded = row_total.astype(jnp.bfloat16)
    row_grad = jnp.dot(row_rounded, projection, preferred_element_type=jnp.float32).astype(
        jnp.bfloat16
    )
    partial_value = lax.dot_general(
        row_rounded, embeddings, (((0,), (0,)), ((), ())), preferred_element_type=jnp.float32
    )
    factor = 1.0 / math.sqrt(cotangent.shape[0] * groups * lax.axis_size("dev"))
    weight_total = lax.psum(partial_value, ("group", "dev"))
    return (row_grad, weight_total * factor)


def solution(mesh):
    return jax.shard_map(
        local,
        mesh=mesh,
        in_specs=(
            P(("group", "dev"), None),
            P(),
            P(None, ("group", "dev")),
            P(("group", "dev")),
            P(("group", "dev"), None),
        ),
        out_specs=(P(("group", "dev"), None), P()),
        check_vma=False,
    )
```

profile of v0, /device:TPU:0, one launch (start us, length us, event | category | flops | bytes accessed | tf_op | source)
XLA Modules:
  0.0 261.9 jit_solution(1550141987545258433)
XLA Ops:
  7.2 0.0 copy-start
  7.2 5.3 %all-to-all-start = ((s32[4,1,128]{2,1,0:T(1,128)}), s32[4,1,128]{2,1,0:T(1,128)S(1)}, u32[]{:S(2)}, u32[]{:S(2)}) async-start(s32[4,1,128]{2,1,0:T(1,128)} %bitcast.30), calls=%async_computation | async-start | bytes 4096 | tf_op jit(solution)/shard_map/all_to_all | solution.py:41
  12.5 0.9 compare_select_fusion.1
  13.4 0.0 copy-start.3
  13.4 0.6 copy-done.3
  14.0 0.6 broadcast_clamp_fusion.2
  14.6 0.0 copy-done
  14.6 1.7 convolution_convert_fusion.1
  16.3 0.6 broadcast_clamp_fusion.1
  16.9 0.2 all-to-all-done
  17.1 0.0 copy-start.7
  17.1 2.6 gather_fusion
  19.7 0.0 copy-done.7
  19.7 4.0 %all-to-all-start.1 = ((bf16[4,128,256]{2,1,0:T(8,128)(2,1)}), bf16[4,128,256]{2,1,0:T(8,128)(2,1)S(1)}, u32[]{:S(2)}, u32[]{:S(2)}) async-start(bf16[4,128,256]{2,1,0:T(8,128)(2,1)} %bitcast.4), calls=%async_computation.1 | async-start | bytes 524288 | tf_op jit(solution)/shard_map/all_to_all | solution.py:44
  23.7 0.6 broadcast_clamp_fusion
  24.3 4.8 %all-to-all-done.1 = bf16[4,128,256]{2,1,0:T(8,128)(2,1)S(1)} async-done(((bf16[4,128,256]{2,1,0:T(8,128)(2,1)}), bf16[4,128,256]{2,1,0:T(8,128)(2,1)S(1)}, u32[]{:S(2)}, u32[]{:S(2)}) %all-to-all-start.1) | async-done | bytes 262176 | tf_op jit(solution)/shard_map/all_to_all | solution.py:44
  29.1 0.0 copy-start.2
  29.1 0.7 copy-done.2
  29.8 1.0 pad_maximum_fusion
  30.8 0.0 copy-start.5
  30.8 9.8 %gather_fusion.1 = bf16[2048,256]{1,0:T(8,128)(2,1)} fusion(bf16[1792,256]{1,0:T(8,128)(2,1)S(1)} %pad_maximum_fusion, s32[2048]{0:T(1024)} %broadcast_clamp_fusion.2), kind=kCustom, calls=%fused_computation.1 | custom fusion | bytes 2105344 | tf_op jit(solution)/shard_map/gather | solution.py:14
  40.6 0.0 copy-done.5
  40.6 0.0 copy-start.4
  40.6 9.0 %gather_fusion.3 = bf16[2048,256]{1,0:T(8,128)(2,1)} fusion(bf16[1792,256]{1,0:T(8,128)(2,1)S(1)} %pad_maximum_fusion, s32[2048]{0:T(1024)S(1)} %copy-done.5), kind=kCustom, calls=%fused_computation.3 | custom fusion | bytes 2105344 | tf_op jit(solution)/shard_map/gather | solution.py:16
  49.6 0.0 copy-done.4
  49.6 9.0 %gather_fusion.2 = bf16[2048,256]{1,0:T(8,128)(2,1)} fusion(bf16[1792,256]{1,0:T(8,128)(2,1)S(1)} %pad_maximum_fusion, s32[2048]{0:T(1024)S(1)} %copy-done.4), kind=kCustom, calls=%fused_computation.2 | custom fusion | bytes 2105344 | tf_op jit(solution)/shard_map/gather | solution.py:15
  58.6 0.0 copy-start.6
  58.6 0.0 copy-start.1
  58.6 2.9 %multiply_reduce_fusion.1 = (f32[2048]{0:T(1024)S(1)}, f32[2048]{0:T(1024)S(1)}) fusion(bf16[2048,256]{1,0:T(8,128)(2,1)} %gather_fusion.2, bf16[2048,256]{1,0:T(8,128)(2,1)} %gather_fusion.1, bf16[2048,256]{1,0:T(8,128)(2,1)} %gather_fusion.3), kind=kLoop, calls=%fused_computation.17 | loop fusion | flops 4714496 | bytes 3162112 | tf_op jit(solution)/shard_map/reduce_sum | solution.py:19
  61.5 0.0 copy-done.6
  61.5 0.0 copy-done.1
  61.5 14.5 %scatter_custom_fusion = f32[1792,256]{1,0:T(8,128)} fusion(s32[2048]{0:T(1024)} %bitcast.27, bf16[2048,256]{1,0:T(8,128)(2,1)} %gather_fusion.3, bf16[2048,256]{1,0:T(8,128)(2,1)S(1)} %copy-done.1, bf16[2048,256]{1,0:T(8,128)(2,1)} %gather_fusion.2, f32[2048]{0:T(1024)S(1)} %get-tuple-element.8, f32[2048]{0:T(1024)S(1)} %get-tuple-element.7, ...), kind=kCustom, calls=%fused_computation.14 | custom fusion | flops 4718592 | bytes 4997632 | tf_op jit(solution)/shard_map/scatter-add | solution.py:27
  76.1 15.7 %scatter_custom_fusion.1 = f32[1792,256]{1,0:T(8,128)} fusion(f32[1792,256]{1,0:T(8,128)} %scatter_custom_fusion, s32[2048]{0:T(1024)S(1)} %bitcast.25, bf16[2048,256]{1,0:T(8,128)(2,1)} %gather_fusion.2, bf16[2048,256]{1,0:T(8,128)(2,1)S(1)} %copy-done.1, f32[2048]{0:T(1024)S(1)} %get-tuple-element.7), kind=kCustom, calls=%fused_computation.12 | custom fusion | flops 3145728 | bytes 3940352 | tf_op jit(solution)/shard_map/scatter-add | solution.py:28
  91.8 15.7 %scatter_custom_fusion.2 = f32[1792,256]{1,0:T(8,128)} fusion(f32[1792,256]{1,0:T(8,128)} %scatter_custom_fusion.1, s32[2048]{0:T(1024)S(1)} %bitcast.23, bf16[2048,256]{1,0:T(8,128)(2,1)} %gather_fusion.3, bf16[2048,256]{1,0:T(8,128)(2,1)S(1)} %copy-done.1, f32[2048]{0:T(1024)S(1)} %get-tuple-element.8), kind=kCustom, calls=%fused_computation.20 | custom fusion | flops 2621440 | bytes 3940352 | tf_op jit(solution)/shard_map/scatter-add | solution.py:29
  107.5 1.8 slice.38
  109.2 3.4 %all-to-all-start.2 = ((bf16[4,128,256]{2,1,0:T(8,128)(2,1)}), bf16[4,128,256]{2,1,0:T(8,128)(2,1)S(1)}, u32[]{:S(2)}, u32[]{:S(2)}) async-start(bf16[4,128,256]{2,1,0:T(8,128)(2,1)} %bitcast.10), calls=%async_computation.2 | async-start | bytes 524288 | tf_op jit(solution)/shard_map/all_to_all | solution.py:48
  112.6 0.0 all-reduce.2.cloned.1.call-start
  112.7 1.4 slice.32
  114.1 3.9 %all-to-all-done.2 = bf16[4,128,256]{2,1,0:T(8,128)(2,1)S(1)} async-done(((bf16[4,128,256]{2,1,0:T(8,128)(2,1)}), bf16[4,128,256]{2,1,0:T(8,128)(2,1)S(1)}, u32[]{:S(2)}, u32[]{:S(2)}) %all-to-all-start.2) | async-done | bytes 262176 | tf_op jit(solution)/shard_map/all_to_all | solution.py:48
  118.0 4.2 %scatter_custom_fusion.3 = f32[1280,256]{1,0:T(8,128)S(1)} fusion(f32[1280,256]{1,0:T(8,128)S(1)} %slice.32, s32[512]{0:T(512)} %bitcast.29, bf16[512,256]{1,0:T(8,128)(2,1)S(1)} %bitcast.21), kind=kCustom, calls=%fused_computation.28 | custom fusion | flops 262144 | bytes 1572864 | tf_op jit(solution)/shard_map/scatter-add | solution.py:52
  122.2 1.6 fusion.18
  123.8 0.0 all-reduce.2.cloned.1.call-update
  123.8 2.9 %convolution_convert_fusion = bf16[1280,768]{1,0:T(8,128)(2,1)} fusion(bf16[256,768]{1,0:T(8,128)(2,1)} %param.6, f32[1280,256]{1,0:T(8,128)S(1)} %scatter_custom_fusion.3), kind=kOutput, calls=%fused_computation.8 | convolution fusion | flops 504627200 | bytes 3670016 | tf_op jit(solution)/shard_map/dot_general | solution.py:55
  126.8 126.2 %all-reduce.2.cloned.1.call-done = f32[256,768]{1,0:T(8,128)} async-done(((f32[256,768]{1,0:T(8,128)}), f32[256,768]{1,0:T(8,128)}) %all-reduce.2.cloned.1.call-update) | async-done | bytes 786448 | tf_op jit(solution)/shard_map/psum | solution.py:62
  253.0 2.1 broadcast_multiply_fusion
  (3 shorter events, 0.0 us)
Async XLA Ops:
  7.2 7.4 %copy-start = (bf16[1280,768]{1,0:T(8,128)(2,1)S(1)}, bf16[1280,768]{1,0:T(8,128)(2,1)}, u32[]{:S(2)}) copy-start(bf16[1280,768]{1,0:T(8,128)(2,1)} %param.5) | copy-start | bytes 5898244
  7.2 9.9 %all-to-all-start = ((s32[4,1,128]{2,1,0:T(1,128)}), s32[4,1,128]{2,1,0:T(1,128)S(1)}, u32[]{:S(2)}, u32[]{:S(2)}) async-start(s32[4,1,128]{2,1,0:T(1,128)} %bitcast.30), calls=%async_computation | async-start | bytes 4096 | tf_op jit(solution)/shard_map/all_to_all | solution.py:41
  13.4 0.6 copy-start.3
  17.1 2.6 copy-start.7
  19.7 9.4 %all-to-all-start.1 = ((bf16[4,128,256]{2,1,0:T(8,128)(2,1)}), bf16[4,128,256]{2,1,0:T(8,128)(2,1)S(1)}, u32[]{:S(2)}, u32[]{:S(2)}) async-start(bf16[4,128,256]{2,1,0:T(8,128)(2,1)} %bitcast.4), calls=%async_computation.1 | async-start | bytes 524288 | tf_op jit(solution)/shard_map/all_to_all | solution.py:44
  29.1 0.7 copy-start.2
  30.8 9.8 %copy-start.5 = (s32[2048]{0:T(1024)S(1)}, s32[2048]{0:T(1024)}, u32[]{:S(2)}) copy-start(s32[2048]{0:T(1024)} %broadcast_clamp_fusion) | copy-start | bytes 24580
  40.6 9.0 %copy-start.4 = (s32[2048]{0:T(1024)S(1)}, s32[2048]{0:T(1024)}, u32[]{:S(2)}) copy-start(s32[2048]{0:T(1024)} %broadcast_clamp_fusion.1) | copy-start | bytes 24580
  58.6 2.9 %copy-start.6 = (f32[2048]{0:T(1024)S(1)}, f32[2048]{0:T(1024)}, u32[]{:S(2)}) copy-start(f32[2048]{0:T(1024)} %param.8) | copy-start | bytes 24580
  58.6 2.9 %copy-start.1 = (bf16[2048,256]{1,0:T(8,128)(2,1)S(1)}, bf16[2048,256]{1,0:T(8,128)(2,1)}, u32[]{:S(2)}) copy-start(bf16[2048,256]{1,0:T(8,128)(2,1)} %gather_fusion.1) | copy-start | bytes 3145732
  109.2 8.8 %all-to-all-start.2 = ((bf16[4,128,256]{2,1,0:T(8,128)(2,1)}), bf16[4,128,256]{2,1,0:T(8,128)(2,1)S(1)}, u32[]{:S(2)}, u32[]{:S(2)}) async-start(bf16[4,128,256]{2,1,0:T(8,128)(2,1)} %bitcast.10), calls=%async_computation.2 | async-start | bytes 524288 | tf_op jit(solution)/shard_map/all_to_all | solution.py:48
  112.6 140.4 %all-reduce.2.cloned.1.call-start = ((), (), s32[]{:S(2)}) async-start(), calls=%async_computation.3 | async-start | bytes 1572864 | tf_op jit(solution)/shard_map/psum | solution.py:62
Sparse Core Ops, SparseCore 0:
  124.0 129.0 all-reduce.1
where the time goes:
time: 263 us; the launch traced here: 262 us
  waiting for transfers between devices  135 us (51%)
  other arithmetic  58.9 us (22%)
  local copies, waits for them, and re-layouts  34.8 us (13%)
  between operations  14.1 us (5%)
  starting transfers between devices  12.8 us (5%)
  matrix products  6.24 us (2%)
    psum x1, waiting for transfers between devices, local(): weight_total = lax.psum(partial_value, ('group', 'dev'))  126 us
    scatter-add x1, other arithmetic, triplet_gradients(): gradient = gradient.at[triple[1]].add(-pull_term)  15.7 us
    scatter-add x1, other arithmetic, triplet_gradients(): gradient = gradient.at[triple[2]].add(push_term)  15.7 us
    scatter-add x1, other arithmetic, triplet_gradients(): gradient = gradient.at[triple[0]].add(pull_term - push_term)  14.5 us
    gather x1, local copies, waits for them, and re-layouts, triplet_gradients(): anchor_rows = lookup[triple[0]].astype(jnp.float32)  9.79 us
    gather x1, local copies, waits for them, and re-layouts, triplet_gradients(): negative_rows = lookup[triple[2]].astype(jnp.float32)  9 us
    gather x1, local copies, waits for them, and re-layouts, triplet_gradients(): positive_rows = lookup[triple[1]].astype(jnp.float32)  8.98 us
    all_to_all x1, starting transfers between devices, local(): lax.all_to_all(wanted_rows, 'group', split_axis=0, concat_axis=0, tiled=T...  5.31 us
  transfers between devices with their start and end apart: 4, of which 4 were waited for; matrix products, arithmetic and copies ran while one was open for 3% of the time, Pallas kernels for 0%

commit v1 on v0

v1 whole, which is shorter than its diff:
```python
import functools
import math

import jax
import jax.numpy as jnp
from jax import lax
from jax.experimental import pallas as pl
from jax.experimental.pallas import tpu as pltpu
from jax.sharding import PartitionSpec as P

distance_scale = 0.0625
margin = 1.0
pull_share = 0.5

MESH = pl.DeviceIdType.MESH
TILE = 256
NT = (((1,), (1,)), ((), ()))
TN = (((0,), (0,)), ((), ()))


def matmul(left, right, numbers=(((1,), (0,)), ((), ()))):
    return lax.dot_general(left, right, numbers, preferred_element_type=jnp.float32)


def indicator(hit):
    return jnp.where(hit, 1.0, 0.0)


def kernel(
    groups, layers, factor,
    emb_hbm, proj_ref, trip_ref, cot_ref, want_ref,
    row_hbm, weight_ref,
    emb, table, wanted, picks, served, fetched, fetched_flat,
    diff_pos, diff_neg, to_pos, to_neg, term_pos, term_neg,
    grad_own, grad_sent, grad_back, back_flat, rounded, row_out,
    partial, sent1, got1, sum2, sent2, got2, got3, final,
    load_sem, store_sem, want_send, want_recv, row_send, row_recv, back_send, back_recv,
    send1, recv1, send2, recv2, send3, recv3, send4, recv4, send5, recv5,
):
    shard_rows = emb.shape[0]
    rank = proj_ref.shape[0]
    triples = cot_ref.shape[1]
    slots = want_ref.shape[2]
    own_blocks = shard_rows // TILE
    far_blocks = groups * slots // TILE
    trip_blocks = triples // TILE
    pieces = final.shape[2]

    g = lax.axis_index("group")
    d = lax.axis_index("dev")
    z = d // 2
    core = d % 2
    sibling = z * 2 + (1 - core)

    load = pltpu.make_async_copy(emb_hbm, emb, load_sem)
    load.start()

    def peer_of(k):
        return lax.rem(g + k, groups)

    def layer_of(k):
        return lax.rem(z + k, layers)

    barrier = pltpu.get_barrier_semaphore()
    for k in range(1, groups):
        pl.semaphore_signal(barrier, inc=1, device_id=(peer_of(k), d), device_id_type=MESH)
    for k in range(1, layers):
        pl.semaphore_signal(
            barrier, inc=1, device_id=(g, layer_of(k) * 2 + core), device_id_type=MESH
        )
    pl.semaphore_signal(barrier, inc=1, device_id=(g, sibling), device_id_type=MESH)
    pl.semaphore_wait(barrier, groups - 1 + layers - 1 + 1)

    def send(source, target, send_sem, recv_sem, device):
        copy = pltpu.make_async_remote_copy(
            src_ref=source, dst_ref=target, send_sem=send_sem, recv_sem=recv_sem,
            device_id=device, device_id_type=MESH,
        )
        copy.start()
        return copy

    pending = []

    want_copies = []
    for k in range(1, groups):
        want_copies.append(send(
            want_ref.at[peer_of(k)], wanted.at[g], want_send.at[k], want_recv.at[k],
            (peer_of(k), d)))
    wanted[g] = want_ref[g]
    pending += want_copies

    load.wait()

    @pl.loop(0, own_blocks)
    def _(b):
        span = pl.ds(pl.multiple_of(b * TILE, TILE), TILE)
        table[:, span] = matmul(proj_ref[...], emb[span, :], NT).astype(jnp.bfloat16)

    for copy in want_copies:
        copy.wait_recv()

    @pl.loop(0, groups)
    def _(h):
        asked = jnp.maximum(wanted[h], 0)
        place = lax.broadcasted_iota(jnp.int32, (shard_rows, slots), 0)
        picks[h] = indicator(place == asked).astype(jnp.bfloat16)
        served[h] = matmul(table[:, :shard_rows], picks[h]).astype(jnp.bfloat16)

    row_copies = []
    for k in range(1, groups):
        row_copies.append(send(
            served.at[peer_of(k)], fetched.at[g], row_send.at[k], row_recv.at[k],
            (peer_of(k), d)))
    fetched[g] = served[g]
    pending += row_copies

    @pl.loop(0, trip_blocks)
    def _(t):
        cols = pl.ds(pl.multiple_of(t * TILE, TILE), TILE)
        anchor = trip_ref[0:1, cols]
        positive = trip_ref[1:2, cols]
        negative = trip_ref[2:3, cols]
        place = lax.broadcasted_iota(jnp.int32, (TILE, TILE), 0)

        @pl.loop(0, own_blocks)
        def _(b):
            first = pl.multiple_of(b * TILE, TILE)
            at_anchor = indicator(place == anchor - first)
            diff_pos[pl.ds(first, TILE), cols] = (
                at_anchor - indicator(place == positive - first)).astype(jnp.bfloat16)
            diff_neg[pl.ds(first, TILE), cols] = (
                at_anchor - indicator(place == negative - first)).astype(jnp.bfloat16)

        @pl.loop(own_blocks, own_blocks + far_blocks)
        def _(b):
            first = pl.multiple_of(b * TILE, TILE)
            diff_pos[pl.ds(first, TILE), cols] = (
                -indicator(place == positive - first)).astype(jnp.bfloat16)
            diff_neg[pl.ds(first, TILE), cols] = (
                -indicator(place == negative - first)).astype(jnp.bfloat16)

        to_pos[:, cols] = matmul(table[...], diff_pos[:shard_rows, cols])
        to_neg[:, cols] = matmul(table[...], diff_neg[:shard_rows, cols])

    for copy in row_copies:
        copy.wait_recv()
    for h in range(groups):
        fetched_flat[:, h * slots:(h + 1) * slots] = fetched[h]

    @pl.loop(0, trip_blocks)
    def _(t):
        cols = pl.ds(pl.multiple_of(t * TILE, TILE), TILE)
        toward = to_pos[:, cols] + matmul(fetched_flat[...], diff_pos[shard_rows:, cols])
        away = to_neg[:, cols] + matmul(fetched_flat[...], diff_neg[shard_rows:, cols])
        near = distance_scale * jnp.sum(toward * toward, axis=0, keepdims=True)
        far = distance_scale * jnp.sum(away * away, axis=0, keepdims=True)
        gate = jax.nn.sigmoid(margin + near - far)
        weight = 2.0 * distance_scale * cot_ref[:, cols]
        pull = weight * (1.0 - pull_share + pull_share * gate)
        push = weight * pull_share * gate
        term_pos[:, cols] = (pull * toward).astype(jnp.bfloat16)
        term_neg[:, cols] = (-push * away).astype(jnp.bfloat16)

    def scattered(b):
        rows = pl.ds(pl.multiple_of(b * TILE, TILE), TILE)
        return matmul(term_pos[...], diff_pos[rows, :], NT) + matmul(
            term_neg[...], diff_neg[rows, :], NT)

    each = TILE // slots

    @pl.loop(0, far_blocks)
    def _(b):
        block = scattered(b + own_blocks).astype(jnp.bfloat16)
        for part in range(each):
            grad_sent[b * each + part] = block[:, part * slots:(part + 1) * slots]

    back_copies = []
    for k in range(1, groups):
        back_copies.append(send(
            grad_sent.at[peer_of(k)], grad_back.at[g], back_send.at[k], back_recv.at[k],
            (peer_of(k), d)))
    grad_back[g] = grad_sent[g]
    pending += back_copies

    @pl.loop(0, own_blocks)
    def _(b):
        grad_own[b] = scattered(b)

    for copy in back_copies:
        copy.wait_recv()
    for h in range(groups):
        back_flat[:, h * slots:(h + 1) * slots] = grad_back[h]

    half = rank // 2
    partial[...] = jnp.zeros_like(partial)

    @pl.loop(0, own_blocks)
    def _(b):
        rows = pl.ds(pl.multiple_of(b * TILE, TILE), TILE)
        total = grad_own[b]
        for h in range(groups):
            total = total + matmul(grad_back[h], picks[h, rows, :], NT)
        block = total.astype(jnp.bfloat16)
        rounded[b] = block
        for part in range(2):
            partial[part] += matmul(block[part * half:(part + 1) * half, :], emb[rows, :])

    width = partial.shape[2] // 2
    bands = half // 16

    def cut(value):
        return [
            value[:, side * width:(side + 1) * width].reshape(bands, 16, width)
            for side in range(2)
        ]

    for side, value in enumerate(cut(partial[1 - core].astype(jnp.bfloat16))):
        sent1[side * bands:(side + 1) * bands] = value
    copy1 = send(sent1, got1, send1, recv1, (g, sibling))
    pending.append(copy1)

    def row_block(b):
        row_out[b] = matmul(rounded[b], proj_ref[...], TN).astype(jnp.bfloat16)
        rows = pl.ds(b * TILE, TILE)
        store = pltpu.make_async_copy(row_out.at[b], row_hbm.at[rows, :], store_sem.at[b])
        store.start()
        return store

    stores = [row_block(0)]
    kept = cut(partial[core])
    copy1.wait_recv()
    for side in range(2):
        whole = kept[side] + got1[side * bands:(side + 1) * bands].astype(jnp.float32)
        for band in range(bands):
            index = side * bands + band
            sum2[index // pieces, index % pieces] = whole[band]
            sent2[index // pieces, index % pieces] = whole[band].astype(jnp.bfloat16)

    copies2 = []
    for k in range(1, groups):
        copies2.append(send(
            sent2.at[peer_of(k)], got2.at[k], send2.at[k], recv2.at[k], (peer_of(k), d)))
    pending += copies2
    stores += [row_block(b) for b in range(1, (own_blocks + 1) // 2)]
    share = sum2[g]
    for k in range(1, groups):
        copies2[k - 1].wait_recv()
        share = share + got2[k].astype(jnp.float32)

    got3[z] = share.astype(jnp.bfloat16)
    copies3 = []
    for k in range(1, layers):
        copies3.append(send(
            got3.at[z], got3.at[z], send3.at[k], recv3.at[k], (g, layer_of(k) * 2 + core)))
    pending += copies3
    stores += [row_block(b) for b in range((own_blocks + 1) // 2, own_blocks)]
    for copy in copies3:
        copy.wait_recv()
    share = got3[0].astype(jnp.float32)
    for other in range(1, layers):
        share = share + got3[other].astype(jnp.float32)

    final[core, g] = share.astype(jnp.bfloat16)
    copies4 = []
    for k in range(1, groups):
        copies4.append(send(
            final.at[core, g], final.at[core, g], send4.at[k], recv4.at[k], (peer_of(k), d)))
    pending += copies4
    copies5 = []
    for k in range(groups):
        if k:
            copies4[k - 1].wait_recv()
        owner = lax.rem(g + groups - k, groups)
        copies5.append(send(
            final.at[core, owner], final.at[core, owner], send5.at[k], recv5.at[k],
            (g, sibling)))
    pending += copies5
    for copy in copies5:
        copy.wait_recv()
    for part in range(2):
        for index in range(2 * bands):
            side, band = index // bands, index % bands
            first = part * half + band * 16
            weight_ref[first:first + 16, side * width:(side + 1) * width] = (
                final[part, index // pieces, index % pieces].astype(jnp.float32) * factor)

    for store in stores:
        store.wait()
    for copy in pending:
        copy.wait_send()


def local(embeddings, projection, triplets, cotangent, wanted_rows):
    shard_rows, width = embeddings.shape
    rank = projection.shape[0]
    triples = cotangent.shape[0]
    groups = lax.axis_size("group")
    members = lax.axis_size("dev")
    layers = members // 2
    slots = wanted_rows.shape[1]
    table_rows = shard_rows + groups * slots
    bands = rank // 32
    pieces = 2 * bands // groups
    factor = 1.0 / math.sqrt(triples * groups * members)
    bf16, f32 = jnp.bfloat16, jnp.float32
    dma = pltpu.SemaphoreType.DMA
    share = (pieces, 16, width // 2)
    vmem = pltpu.VMEM
    scratch = [
        vmem((shard_rows, width), bf16),
        vmem((rank, shard_rows), bf16),
        vmem((groups, 1, slots), jnp.int32),
        vmem((groups, shard_rows, slots), bf16),
        vmem((groups, rank, slots), bf16),
        vmem((groups, rank, slots), bf16),
        vmem((rank, groups * slots), bf16),
        vmem((table_rows, triples), bf16),
        vmem((table_rows, triples), bf16),
        vmem((rank, triples), f32),
        vmem((rank, triples), f32),
        vmem((rank, triples), bf16),
        vmem((rank, triples), bf16),
        vmem((shard_rows // TILE, rank, TILE), f32),
        vmem((groups, rank, slots), bf16),
        vmem((groups, rank, slots), bf16),
        vmem((rank, groups * slots), bf16),
        vmem((shard_rows // TILE, rank, TILE), bf16),
        vmem((shard_rows // TILE, TILE, width), bf16),
        vmem((2, rank // 2, width), f32),
        vmem((2 * bands, 16, width // 2), bf16),
        vmem((2 * bands, 16, width // 2), bf16),
        vmem((groups,) + share, f32),
        vmem((groups,) + share, bf16),
        vmem((groups,) + share, bf16),
        vmem((layers,) + share, bf16),
        vmem((2, groups) + share, bf16),
        dma, dma((shard_rows // TILE,)),
        dma((groups,)), dma((groups,)), dma((groups,)), dma((groups,)),
        dma((groups,)), dma((groups,)),
        dma, dma, dma((groups,)), dma((groups,)), dma((layers,)), dma((layers,)),
        dma((groups,)), dma((groups,)), dma((groups,)), dma((groups,)),
    ]
    in_vmem = pl.BlockSpec(memory_space=pltpu.VMEM)
    anywhere = pl.BlockSpec(memory_space=pl.ANY)
    return pl.pallas_call(
        functools.partial(kernel, groups, layers, factor),
        out_shape=(
            jax.ShapeDtypeStruct((shard_rows, width), bf16),
            jax.ShapeDtypeStruct((rank, width), f32),
        ),
        in_specs=[anywhere, in_vmem, in_vmem, in_vmem, in_vmem],
        out_specs=(anywhere, in_vmem),
        scratch_shapes=scratch,
        compiler_params=pltpu.CompilerParams(
            collective_id=0, has_side_effects=True, vmem_limit_bytes=60 * 1024 * 1024
        ),
        cost_estimate=pl.CostEstimate(
            flops=10 * table_rows * triples * rank,
            bytes_accessed=4 * shard_rows * width,
            transcendentals=triples,
        ),
    )(
        embeddings, projection, triplets, cotangent.reshape(1, triples),
        wanted_rows.reshape(groups, 1, slots),
    )


def solution(mesh):
    return jax.shard_map(
        local,
        mesh=mesh,
        in_specs=(
            P(("group", "dev"), None),
            P(),
            P(None, ("group", "dev")),
            P(("group", "dev")),
            P(("group", "dev"), None),
        ),
        out_specs=(P(("group", "dev"), None), P()),
        check_vma=False,
    )
```

time: 263 us -> 54.2 us (0.21)
  waiting for transfers between devices: 135 us -> 0 us
  other arithmetic: 58.9 us -> 0 us
  Pallas kernels: 0 us -> 49.5 us
  local copies, waits for them, and re-layouts: 34.8 us -> 3.9 us
  between operations: 14.1 us -> 0.65 us
  starting transfers between devices: 12.8 us -> 0 us
  matrix products: 6.24 us -> 0 us
    psum x1 -> x0, waiting for transfers between devices: 126 us -> none  [local(): weight_total = lax.psum(partial_value, ('group', 'dev'))]
    scatter-add x4 -> x0, other arithmetic: 50.2 us -> none  [the longest x1 15.7 us: triplet_gradients(): gradient = gradient.at[triple[1]].add(-pull_term)]
    pallas_call x0 -> x1, Pallas kernels: none -> 49.5 us  [local(): pl.pallas_call(functools.partial(kernel, groups, layers, factor), out_sha...]
    gather x4 -> x0, local copies, waits for them, and re-layouts: 30.4 us -> none  [the longest x1 9.79 us: triplet_gradients(): anchor_rows = lookup[triple[0]].astype(jnp.float32)]
    all_to_all x3 -> x0, starting transfers between devices: 12.8 us -> none  [the longest x1 5.31 us: local(): lax.all_to_all(wanted_rows, 'group', split_axis=0, concat_axis=0, tiled=T...]
    all_to_all x3 -> x0, waiting for transfers between devices: 8.82 us -> none  [the longest x1 4.78 us: local(): lax.all_to_all(served, 'group', split_axis=0, concat_axis=0, tiled=True)]
    dot_general x3 -> x0, matrix products: 6.24 us -> none  [the longest x1 2.94 us: local(): jnp.dot(row_rounded, projection, preferred_element_type=jnp.float32)]
    slice x2 -> x0, local copies, waits for them, and re-layouts: 3.17 us -> none  [the longest x1 1.77 us: local(): gradient[shard_rows:].reshape(groups, -1, rank_width).astype(jnp.bfloat16)]
  transfers between devices with their start and end apart: 4 -> 0, of which waited for: 4 -> 0; matrix products, arithmetic and copies ran while one was open for 3% -> 0% of each run, Pallas kernels for 0% -> 0%
where the time goes in v1:
time: 54.2 us; the launch traced here: 54 us
  Pallas kernels  49.5 us (91%)
  local copies, waits for them, and re-layouts  3.9 us (7%)
  between operations  0.65 us (1%)
    pallas_call x1, Pallas kernels, local(): pl.pallas_call(functools.partial(kernel, groups, layers, factor), out_sha...  49.5 us
    unnamed x4, local copies, waits for them, and re-layouts  3.9 us

profile of v1, /device:TPU:0, one launch (start us, length us, event | category | flops | bytes accessed | tf_op | source)
XLA Modules:
  0.0 54.0 jit_solution(5997587407571551862)
XLA Ops:
  0.6 49.5 %shard_map.68 = (bf16[1280,768]{1,0:T(8,128)(2,1)}, f32[256,768]{1,0:T(8,128)}) custom-call(bf16[1280,768]{1,0:T(8,128)(2,1)} %emb_hbm.1, bf16[256,768]{1,0:T(8,128)(2,1)} %proj_ref.1, s32[3,2048]{1,0:T(4,128)} %trip_ref.1, f32[1,2048]{1,0:T(1,128)} %bitcast.2, s32[4,1,128]{2,1,0:T(1,128)} %bitcast.3), custom_call_target="tpu_custom_call" | custom-call | flops 9395240960 | bytes 3932160 | tf_op jit(solution)/shard_map/pallas_call | solution.py:345
  50.1 0.0 copy-start
  50.1 3.0 %copy.9 = bf16[1280,768]{1,0:T(8,128)(2,1)} copy(bf16[1280,768]{1,0:T(8,128)(2,1)} %get-tuple-element.4) | data formatting | bytes 3932160
  53.1 0.0 copy-done
  53.1 0.9 %copy.10 = f32[256,768]{1,0:T(8,128)} copy(f32[256,768]{1,0:T(8,128)S(1)} %copy-done) | data formatting | bytes 1572864
Async XLA Ops:
  50.1 3.0 %copy-start = (f32[256,768]{1,0:T(8,128)S(1)}, f32[256,768]{1,0:T(8,128)}, u32[]{:S(2)}) copy-start(f32[256,768]{1,0:T(8,128)} %get-tuple-element.5) | copy-start | bytes 2359300

commit v2 on v0

v2 whole, which is shorter than its diff:
```python
import functools
import math

import jax
import jax.numpy as jnp
from jax import lax
from jax.experimental import pallas as pl
from jax.experimental.pallas import tpu as pltpu
from jax.sharding import PartitionSpec as P

distance_scale = 0.0625
margin = 1.0
pull_share = 0.5

MESH = pl.DeviceIdType.MESH
TILE = 256
LANES = 128
NT = (((1,), (1,)), ((), ()))


def matmul(left, right, numbers=(((1,), (0,)), ((), ()))):
    return lax.dot_general(left, right, numbers, preferred_element_type=jnp.float32)


def hits(place, index, first):
    return place == (index - first).astype(jnp.float32).astype(jnp.bfloat16)


def kernel(
    groups, layers,
    emb_hbm, proj_hbm, trip_hbm, cot_hbm, want_hbm,
    rounded_hbm, weight_hbm,
    emb, proj, trip, cot, table, wanted, picks, served, fetched, fetched_flat,
    diff, apart, terms, grad_own, grad_sent, grad_back, rounded, turned,
    partial, sent1, got1, sum2, sent2, got2, got3, final, summed,
    load_sem, store_sem, want_send, want_recv, row_send, row_recv, back_send, back_recv,
    send1, recv1, send2, recv2, send3, recv3, send4, recv4, send5, recv5,
):
    shard_rows = emb.shape[0]
    rank = proj.shape[0]
    triples = cot.shape[1]
    slots = wanted.shape[2]
    far_rows = groups * slots
    own_blocks = shard_rows // TILE
    far_blocks = far_rows // TILE
    trip_blocks = triples // TILE
    pieces = final.shape[2]
    bf16, f32 = jnp.bfloat16, jnp.float32

    g = lax.axis_index("group")
    d = lax.axis_index("dev")
    z = d // 2
    core = d % 2
    sibling = z * 2 + (1 - core)

    loads = []
    blocks = [slice(b * TILE, (b + 1) * TILE) for b in range(own_blocks)]
    for number, (source, target) in enumerate([
        (trip_hbm, trip), (want_hbm.at[g], wanted.at[g]), (cot_hbm, cot), (proj_hbm, proj),
    ] + [(emb_hbm.at[rows], emb.at[rows]) for rows in blocks]):
        loads.append(pltpu.make_async_copy(source, target, load_sem.at[number]))
        loads[-1].start()

    def peer_of(k):
        return lax.rem(g + k, groups)

    def layer_of(k):
        return lax.rem(z + k, layers)

    barrier = pltpu.get_barrier_semaphore()
    for k in range(1, groups):
        pl.semaphore_signal(barrier, inc=1, device_id=(peer_of(k), d), device_id_type=MESH)
    for k in range(1, layers):
        pl.semaphore_signal(
            barrier, inc=1, device_id=(g, layer_of(k) * 2 + core), device_id_type=MESH
        )
    pl.semaphore_signal(barrier, inc=1, device_id=(g, sibling), device_id_type=MESH)
    pl.semaphore_wait(barrier, groups - 1 + layers - 1 + 1)

    def send(source, target, send_sem, recv_sem, device):
        copy = pltpu.make_async_remote_copy(
            src_ref=source, dst_ref=target, send_sem=send_sem, recv_sem=recv_sem,
            device_id=device, device_id_type=MESH,
        )
        copy.start()
        return copy

    pending = []

    want_copies = []
    for k in range(1, groups):
        want_copies.append(send(
            want_hbm.at[peer_of(k)], wanted.at[g], want_send.at[k], want_recv.at[k],
            (peer_of(k), d)))
    pending += want_copies

    one = jnp.ones((), bf16)
    zero = jnp.zeros((), bf16)
    for load in loads[:3]:
        load.wait()

    def tile_parts(t):
        cols = pl.ds(pl.multiple_of(t * TILE, TILE), TILE)
        pair = pl.ds(pl.multiple_of(t * 2 * TILE, 2 * TILE), 2 * TILE)
        others = jnp.concatenate([trip[1:2, cols], trip[2:3, cols]], axis=1)
        place = lax.broadcasted_iota(jnp.int32, (TILE, TILE), 0).astype(f32).astype(bf16)
        return cols, pair, others, place, jnp.concatenate([place, place], axis=1)

    @pl.loop(0, trip_blocks)
    def _(t):
        cols, pair, others, place, wide = tile_parts(t)
        for b in range(own_blocks, own_blocks + far_blocks):
            first = b * TILE
            diff[first:first + TILE, pair] = jnp.where(hits(wide, others, first), -one, zero)

    loads[3].wait()
    for rows, load in zip(blocks, loads[4:]):
        load.wait()
        table[:, rows] = matmul(proj[...], emb[rows, :], NT).astype(bf16)

    for copy in want_copies:
        copy.wait_recv()

    narrow = lax.broadcasted_iota(jnp.int32, (TILE, slots), 0).astype(f32).astype(bf16)
    for h in range(groups):
        asked = jnp.maximum(wanted[h], 0)
        for b in range(own_blocks):
            picks[b * TILE:(b + 1) * TILE, h * slots:(h + 1) * slots] = jnp.where(
                hits(narrow, asked, b * TILE), one, zero)
    for b in range(far_blocks):
        block = matmul(table[...], picks[:, b * TILE:(b + 1) * TILE]).astype(bf16)
        for part in range(TILE // slots):
            served[b * (TILE // slots) + part] = block[:, part * slots:(part + 1) * slots]

    row_copies = []
    for k in range(1, groups):
        row_copies.append(send(
            served.at[peer_of(k)], fetched.at[g], row_send.at[k], row_recv.at[k],
            (peer_of(k), d)))
    fetched[g] = served[g]
    pending += row_copies

    def own_tile(t):
        cols, pair, others, place, wide = tile_parts(t)
        anchor = trip[0:1, cols]
        total = None
        for b in range(own_blocks):
            first = b * TILE
            at_anchor = jnp.where(hits(place, anchor, first), one, zero)
            block = jnp.concatenate([at_anchor, at_anchor], axis=1) - jnp.where(
                hits(wide, others, first), one, zero)
            diff[first:first + TILE, pair] = block
            term = matmul(table[:, first:first + TILE], block)
            total = term if total is None else total + term
        apart[:, pair] = total

    @pl.loop(0, trip_blocks // 2)
    def _(t):
        own_tile(2 * t)
        own_tile(2 * t + 1)

    for copy in row_copies:
        copy.wait_recv()
    for h in range(groups):
        fetched_flat[:, h * slots:(h + 1) * slots] = fetched[h]

    for t in range(trip_blocks):
        cols = slice(t * TILE, (t + 1) * TILE)
        pair = slice(t * 2 * TILE, (t + 1) * 2 * TILE)
        both = apart[:, pair] + matmul(fetched_flat[...], diff[shard_rows:, pair])
        squares = distance_scale * jnp.sum(both * both, axis=0, keepdims=True)
        gate = jax.nn.sigmoid(margin + squares[:, :TILE] - squares[:, TILE:])
        weight = 2.0 * distance_scale * cot[:, cols]
        pull = weight * (1.0 - pull_share + pull_share * gate)
        push = weight * pull_share * gate
        scale = jnp.concatenate([pull, -push], axis=1)
        terms[pair, :] = jnp.transpose((scale * both).astype(bf16))

    per = min(far_rows, 4 * slots)

    @pl.loop(0, far_rows // per)
    def _(b):
        rows = pl.ds(pl.multiple_of(shard_rows + b * per, slots), per)
        block = matmul(diff[rows, :], terms[...]).astype(bf16)
        grad_sent[pl.ds(b * (per // slots), per // slots)] = block.reshape(
            per // slots, slots, rank)

    back_copies = []
    for k in range(1, groups):
        back_copies.append(send(
            grad_sent.at[peer_of(k)], grad_back.at[g], back_send.at[k], back_recv.at[k],
            (peer_of(k), d)))
    grad_back[g] = grad_sent[g]
    pending += back_copies

    some = shard_rows // 2

    @pl.loop(0, 2)
    def _(b):
        rows = pl.ds(pl.multiple_of(b * some, some), some)
        grad_own[rows, :] = matmul(diff[rows, :], terms[...])

    for copy in back_copies:
        copy.wait_recv()
    returned = grad_back[...].reshape(far_rows, rank)
    for b in range(own_blocks):
        rows = slice(b * TILE, (b + 1) * TILE)
        block = (grad_own[rows, :] + matmul(picks[rows, :], returned)).astype(bf16)
        rounded[rows, :] = block
        turned[:, rows] = jnp.transpose(block)
    stores = [pltpu.make_async_copy(rounded, rounded_hbm, store_sem.at[0])]
    stores[0].start()

    half = rank // 2
    bands = half // 16
    span = 2 * LANES
    parts = range(emb.shape[1] // span)

    def cut(value):
        return [
            value[:, side * LANES:(side + 1) * LANES].reshape(bands, 16, LANES)
            for side in range(2)
        ]

    copies1 = []
    for s in parts:
        product = matmul(turned[...], emb[:, s * span:(s + 1) * span])
        partial[s, 0] = product[:half]
        partial[s, 1] = product[half:]
        for side, value in enumerate(cut(partial[s, 1 - core].astype(bf16))):
            sent1[s, side * bands:(side + 1) * bands] = value
        copies1.append(send(sent1.at[s], got1.at[s], send1.at[s], recv1.at[s], (g, sibling)))
    pending += copies1

    copies2 = {}
    for s in parts:
        kept = cut(partial[s, core])
        copies1[s].wait_recv()
        for side in range(2):
            whole = kept[side] + got1[s, side * bands:(side + 1) * bands].astype(f32)
            for band in range(bands):
                index = side * bands + band
                sum2[s, index // pieces, index % pieces] = whole[band]
                sent2[s, index // pieces, index % pieces] = whole[band].astype(bf16)
        for k in range(1, groups):
            copies2[s, k] = send(
                sent2.at[s, peer_of(k)], got2.at[s, k], send2.at[s, k], recv2.at[s, k],
                (peer_of(k), d))
    pending += list(copies2.values())

    copies3 = {}
    for s in parts:
        share = sum2[s, g]
        for k in range(1, groups):
            copies2[s, k].wait_recv()
            share = share + got2[s, k].astype(f32)
        got3[s, z] = share.astype(bf16)
        for k in range(1, layers):
            copies3[s, k] = send(
                got3.at[s, z], got3.at[s, z], send3.at[s, k], recv3.at[s, k],
                (g, layer_of(k) * 2 + core))
    pending += list(copies3.values())

    copies4 = {}
    copies5 = {}

    def forward(s, k):
        owner = lax.rem(g + groups - k, groups)
        copies5[s, k] = send(
            final.at[s, core, owner], final.at[s, core, owner], send5.at[s, k], recv5.at[s, k],
            (g, sibling))

    for s in parts:
        for k in range(1, layers):
            copies3[s, k].wait_recv()
        share = got3[s, 0].astype(f32)
        for other in range(1, layers):
            share = share + got3[s, other].astype(f32)
        final[s, core, g] = share.astype(bf16)
        for k in range(1, groups):
            copies4[s, k] = send(
                final.at[s, core, g], final.at[s, core, g], send4.at[s, k], recv4.at[s, k],
                (peer_of(k), d))
        forward(s, 0)
    pending += list(copies4.values())
    for s in parts:
        for k in range(1, groups):
            copies4[s, k].wait_recv()
            forward(s, k)
    pending += list(copies5.values())
    for s in parts:
        for k in range(groups):
            copies5[s, k].wait_recv()
        for part in range(2):
            for index in range(2 * bands):
                side, band = index // bands, index % bands
                row = part * half + band * 16
                column = s * span + side * LANES
                summed[row:row + 16, column:column + LANES] = (
                    final[s, part, index // pieces, index % pieces])
        columns = slice(s * span, (s + 1) * span)
        stores.append(pltpu.make_async_copy(
            summed.at[:, columns], weight_hbm.at[:, columns], store_sem.at[1 + s]))
        stores[-1].start()

    for store in stores:
        store.wait()
    for copy in pending:
        copy.wait_send()


def finish_kernel(
    factor, rounded_hbm, proj_hbm, weight_hbm, row_hbm, out_hbm,
    rounded, proj, weight, row, out, proj_sem, in_sem, row_sem, weight_sem, out_sem,
):
    blocks = rounded.shape[0] // TILE

    def copy(source, target, sem):
        made = pltpu.make_async_copy(source, target, sem)
        made.start()
        return made

    proj_load = copy(proj_hbm, proj, proj_sem)
    loads = []
    for b in range(blocks):
        rows = slice(b * TILE, (b + 1) * TILE)
        loads.append(copy(rounded_hbm.at[rows], rounded.at[rows], in_sem.at[b]))
    weight_load = copy(weight_hbm, weight, weight_sem)
    proj_load.wait()
    stores = []
    for b in range(blocks):
        rows = slice(b * TILE, (b + 1) * TILE)
        loads[b].wait()
        row[rows] = matmul(rounded[rows], proj[...]).astype(jnp.bfloat16)
        for part in range(2):
            some = slice(b * TILE + part * LANES, b * TILE + (part + 1) * LANES)
            stores.append(copy(row.at[some], row_hbm.at[some], row_sem.at[2 * b + part]))
    weight_load.wait()
    out[...] = weight[...].astype(jnp.float32) * factor
    stores.append(copy(out, out_hbm, out_sem))
    for store in stores:
        store.wait()


def local(embeddings, projection, triplets, cotangent, wanted_rows):
    shard_rows, width = embeddings.shape
    rank = projection.shape[0]
    triples = cotangent.shape[0]
    groups = lax.axis_size("group")
    members = lax.axis_size("dev")
    layers = members // 2
    slots = wanted_rows.shape[1]
    far_rows = groups * slots
    table_rows = shard_rows + far_rows
    bands = rank // 32
    pieces = 2 * bands // groups
    factor = 1.0 / math.sqrt(triples * groups * members)
    bf16, f32 = jnp.bfloat16, jnp.float32
    dma = pltpu.SemaphoreType.DMA
    share = (pieces, 16, LANES)
    parts = width // (2 * LANES)
    vmem = pltpu.VMEM
    scratch = [
        vmem((shard_rows, width), bf16),
        vmem((rank, width), bf16),
        vmem((3, triples), jnp.int32),
        vmem((1, triples), f32),
        vmem((rank, shard_rows), bf16),
        vmem((groups, 1, slots), jnp.int32),
        vmem((shard_rows, far_rows), bf16),
        vmem((groups, rank, slots), bf16),
        vmem((groups, rank, slots), bf16),
        vmem((rank, far_rows), bf16),
        vmem((table_rows, 2 * triples), bf16),
        vmem((rank, 2 * triples), f32),
        vmem((2 * triples, rank), bf16),
        vmem((shard_rows, rank), f32),
        vmem((groups, slots, rank), bf16),
        vmem((groups, slots, rank), bf16),
        vmem((shard_rows, rank), bf16),
        vmem((rank, shard_rows), bf16),
        vmem((parts, 2, rank // 2, 2 * LANES), f32),
        vmem((parts, 2 * bands, 16, LANES), bf16),
        vmem((parts, 2 * bands, 16, LANES), bf16),
        vmem((parts, groups) + share, f32),
        vmem((parts, groups) + share, bf16),
        vmem((parts, groups) + share, bf16),
        vmem((parts, layers) + share, bf16),
        vmem((parts, 2, groups) + share, bf16),
        vmem((rank, width), bf16),
        dma((4 + shard_rows // TILE,)), dma((1 + parts,)),
        dma((groups,)), dma((groups,)), dma((groups,)), dma((groups,)),
        dma((groups,)), dma((groups,)),
        dma((parts,)), dma((parts,)),
        dma((parts, groups)), dma((parts, groups)), dma((parts, layers)), dma((parts, layers)),
        dma((parts, groups)), dma((parts, groups)), dma((parts, groups)), dma((parts, groups)),
    ]
    anywhere = pl.BlockSpec(memory_space=pl.ANY)
    rounded, weight = pl.pallas_call(
        functools.partial(kernel, groups, layers),
        out_shape=(
            jax.ShapeDtypeStruct((shard_rows, rank), bf16),
            jax.ShapeDtypeStruct((rank, width), bf16),
        ),
        in_specs=[anywhere] * 5,
        out_specs=(anywhere, anywhere),
        scratch_shapes=scratch,
        compiler_params=pltpu.CompilerParams(
            collective_id=0, has_side_effects=True, vmem_limit_bytes=60 * 1024 * 1024
        ),
        cost_estimate=pl.CostEstimate(
            flops=10 * table_rows * triples * rank,
            bytes_accessed=4 * shard_rows * width,
            transcendentals=triples,
        ),
    )(
        embeddings, projection, triplets, cotangent.reshape(1, triples),
        wanted_rows.reshape(groups, 1, slots),
    )
    blocks = shard_rows // TILE
    return pl.pallas_call(
        functools.partial(finish_kernel, factor),
        out_shape=(
            jax.ShapeDtypeStruct((shard_rows, width), bf16),
            jax.ShapeDtypeStruct((rank, width), f32),
        ),
        in_specs=[anywhere] * 3,
        out_specs=(anywhere, anywhere),
        scratch_shapes=[
            vmem((shard_rows, rank), bf16), vmem((rank, width), bf16),
            vmem((rank, width), bf16), vmem((shard_rows, width), bf16),
            vmem((rank, width), f32),
            dma, dma((blocks,)), dma((2 * blocks,)), dma, dma,
        ],
        compiler_params=pltpu.CompilerParams(vmem_limit_bytes=60 * 1024 * 1024),
        cost_estimate=pl.CostEstimate(
            flops=2 * shard_rows * width * rank,
            bytes_accessed=2 * (shard_rows * (width + rank) + 4 * rank * width),
            transcendentals=0,
        ),
    )(rounded, projection, weight)


def solution(mesh):
    return jax.shard_map(
        local,
        mesh=mesh,
        in_specs=(
            P(("group", "dev"), None),
            P(),
            P(None, ("group", "dev")),
            P(("group", "dev")),
            P(("group", "dev"), None),
        ),
        out_specs=(P(("group", "dev"), None), P()),
        check_vma=False,
    )
```

time: 263 us -> 42 us (0.16)
  waiting for transfers between devices: 135 us -> 0 us
  other arithmetic: 58.9 us -> 0 us
  Pallas kernels: 0 us -> 40.5 us
  local copies, waits for them, and re-layouts: 34.8 us -> 0 us
  between operations: 14.1 us -> 0.64 us
  starting transfers between devices: 12.8 us -> 0 us
  matrix products: 6.24 us -> 0 us
    psum x1 -> x0, waiting for transfers between devices: 126 us -> none  [local(): weight_total = lax.psum(partial_value, ('group', 'dev'))]
    scatter-add x4 -> x0, other arithmetic: 50.2 us -> none  [the longest x1 15.7 us: triplet_gradients(): gradient = gradient.at[triple[1]].add(-pull_term)]
    pallas_call x0 -> x2, Pallas kernels: none -> 40.5 us  [the longest x1 36.6 us: local(): pl.pallas_call(functools.partial(kernel, groups, layers), out_shape=(jax....]
    gather x4 -> x0, local copies, waits for them, and re-layouts: 30.4 us -> none  [the longest x1 9.79 us: triplet_gradients(): anchor_rows = lookup[triple[0]].astype(jnp.float32)]
    all_to_all x3 -> x0, starting transfers between devices: 12.8 us -> none  [the longest x1 5.31 us: local(): lax.all_to_all(wanted_rows, 'group', split_axis=0, concat_axis=0, tiled=T...]
    all_to_all x3 -> x0, waiting for transfers between devices: 8.82 us -> none  [the longest x1 4.78 us: local(): lax.all_to_all(served, 'group', split_axis=0, concat_axis=0, tiled=True)]
    dot_general x3 -> x0, matrix products: 6.24 us -> none  [the longest x1 2.94 us: local(): jnp.dot(row_rounded, projection, preferred_element_type=jnp.float32)]
    slice x2 -> x0, local copies, waits for them, and re-layouts: 3.17 us -> none  [the longest x1 1.77 us: local(): gradient[shard_rows:].reshape(groups, -1, rank_width).astype(jnp.bfloat16)]
  transfers between devices with their start and end apart: 4 -> 0, of which waited for: 4 -> 0; matrix products, arithmetic and copies ran while one was open for 3% -> 0% of each run, Pallas kernels for 0% -> 0%
where the time goes in v2:
time: 42 us; the launch traced here: 41.1 us
  Pallas kernels  40.5 us (96%)
  between operations  0.64 us (2%)
    pallas_call x1, Pallas kernels, local(): pl.pallas_call(functools.partial(kernel, groups, layers), out_shape=(jax....  36.6 us
    pallas_call x1, Pallas kernels, local(): pl.pallas_call(functools.partial(finish_kernel, factor), out_shape=(jax.S...  3.89 us

profile of v2, /device:TPU:0, one launch (start us, length us, event | category | flops | bytes accessed | tf_op | source)
XLA Modules:
  0.0 41.1 jit_solution(120787043871931945)
XLA Ops:
  0.6 36.6 %shard_map.68 = (bf16[1280,256]{1,0:T(8,128)(2,1)}, bf16[256,768]{1,0:T(8,128)(2,1)}) custom-call(bf16[1280,768]{1,0:T(8,128)(2,1)} %emb_hbm.1, bf16[256,768]{1,0:T(8,128)(2,1)} %proj_hbm.3, s32[3,2048]{1,0:T(4,128)} %trip_hbm.1, f32[1,2048]{1,0:T(1,128)} %bitcast.2, s32[4,1,128]{2,1,0:T(1,128)} %bitcast.3), custom_call_target="tpu_custom_call" | custom-call | flops 9395240960 | bytes 3932160 | tf_op jit(solution)/shard_map/pallas_call | solution.py:399
  37.2 3.9 %shard_map.69 = (bf16[1280,768]{1,0:T(8,128)(2,1)}, f32[256,768]{1,0:T(8,128)}) custom-call(bf16[1280,256]{1,0:T(8,128)(2,1)} %get-tuple-element.4.rounded_hbm, bf16[256,768]{1,0:T(8,128)(2,1)} %proj_hbm.3, bf16[256,768]{1,0:T(8,128)(2,1)} %get-tuple-element.5.weight_hbm), custom_call_target="tpu_custom_call" | custom-call | flops 503316480 | bytes 4194304 | tf_op jit(solution)/shard_map/pallas_call | solution.py:421

commit v3 on v2

--- a/solution.py
+++ b/solution.py
@@ -193,12 +193,7 @@
     grad_back[g] = grad_sent[g]
     pending += back_copies
 
-    some = shard_rows // 2
-
-    @pl.loop(0, 2)
-    def _(b):
-        rows = pl.ds(pl.multiple_of(b * some, some), some)
-        grad_own[rows, :] = matmul(diff[rows, :], terms[...])
+    grad_own[...] = matmul(diff[:shard_rows, :], terms[...])
 
     for copy in back_copies:
         copy.wait_recv()

time: 42 us -> 43.1 us (1.026)
  Pallas kernels: 40.5 us -> 41.6 us
    pallas_call x1, Pallas kernels: 36.6 us -> 37.7 us  [local(): pl.pallas_call(functools.partial(kernel, groups, layers), out_shape=(jax....]
where the time goes in v3:
time: 43.1 us; the launch traced here: 42.3 us
  Pallas kernels  41.6 us (97%)
  between operations  0.64 us (1%)
    pallas_call x1, Pallas kernels, local(): pl.pallas_call(functools.partial(kernel, groups, layers), out_shape=(jax....  37.7 us
    pallas_call x1, Pallas kernels, local(): pl.pallas_call(functools.partial(finish_kernel, factor), out_shape=(jax.S...  3.9 us

profile of v3, /device:TPU:0, one launch (start us, length us, event | category | flops | bytes accessed | tf_op | source)
XLA Modules:
  0.0 42.3 jit_solution(7799999783432772947)
XLA Ops:
  0.6 37.7 %shard_map.68 = (bf16[1280,256]{1,0:T(8,128)(2,1)}, bf16[256,768]{1,0:T(8,128)(2,1)}) custom-call(bf16[1280,768]{1,0:T(8,128)(2,1)} %emb_hbm.1, bf16[256,768]{1,0:T(8,128)(2,1)} %proj_hbm.3, s32[3,2048]{1,0:T(4,128)} %trip_hbm.1, f32[1,2048]{1,0:T(1,128)} %bitcast.2, s32[4,1,128]{2,1,0:T(1,128)} %bitcast.3), custom_call_target="tpu_custom_call" | custom-call | flops 9395240960 | bytes 3932160 | tf_op jit(solution)/shard_map/pallas_call | solution.py:394
  38.4 3.9 %shard_map.69 = (bf16[1280,768]{1,0:T(8,128)(2,1)}, f32[256,768]{1,0:T(8,128)}) custom-call(bf16[1280,256]{1,0:T(8,128)(2,1)} %get-tuple-element.4.rounded_hbm, bf16[256,768]{1,0:T(8,128)(2,1)} %proj_hbm.3, bf16[256,768]{1,0:T(8,128)(2,1)} %get-tuple-element.5.weight_hbm), custom_call_target="tpu_custom_call" | custom-call | flops 503316480 | bytes 4194304 | tf_op jit(solution)/shard_map/pallas_call | solution.py:416
